TPU v7x, 512 devices: a whole 4x8x8 slice. The times are simulated.
512 devices in a mesh: ct: 128 (over y, z, core), bl: 4 (over x).
Axes of the slice: x: 4, y: 8, z: 8, core: 2. Of those that a mesh axis runs over, the one named last changes fastest.
Arguments:
- samples: bfloat16 [1024, 65536], P('ct', 'bl'), may hold values from -6 to 6
- history: bfloat16 [1024, 1536], P('ct'), may hold values from -6 to 6
- tile_cell: int32 [256, 36], P('ct'), may hold values from 0 to 7
- tile_weight: float32 [256, 36], P('ct'), may hold values from 0.25 to 4
Outputs:
- grid: float32 [8, 256, 2, 128, 128], P('bl', 'ct')
All inputs are finite; a program needn't handle non-finite values.
Results may differ from a plain program's by a relative error of at most 0.0048.
Values may be sent and summed in bfloat16 or wider, within the bound.
A program may use at most 64 MiB of HBM per device.

v0:
```python
import math
import jax
import jax.numpy as jnp
from jax import lax
from jax.sharding import PartitionSpec as P

CH = 256
BLOCK = 128
TAPS = 4
SPECTRA = 128
CELL_DEV = 2
FRAME = 512


def from_behind(value, axis, by):
    size = lax.axis_size(axis)
    pairs = [(i, i + by) for i in range(size) if 0 <= i + by < size]
    return lax.ppermute(value, axis, pairs)


def filter_table():
    span = TAPS * FRAME
    sample_pos = jnp.arange(span, dtype=jnp.float32) + 0.5
    window = jnp.sinc(sample_pos / FRAME - TAPS / 2.0) * (
        0.5 - 0.5 * jnp.cos(2.0 * math.pi * sample_pos / span)
    )
    phase_int = (
        jnp.arange(FRAME, dtype=jnp.int32)[:, None]
        * jnp.arange(CH, dtype=jnp.int32)[None, :]
        % FRAME
    )
    angle = phase_int.astype(jnp.float32) * (2.0 * math.pi / FRAME)
    basis = jnp.concatenate([jnp.cos(angle), -jnp.sin(angle)], axis=1)
    table = window.reshape(TAPS, FRAME)[:, :, None] * basis[None] * (2.0 / math.sqrt(FRAME))
    return table.astype(jnp.bfloat16)


def cell_selector(tile_cell, weights, tri_index, is_valid, cell_count):
    picked = jnp.take(tile_cell, tri_index, axis=1)
    picked_weight = jnp.take(weights, tri_index, axis=1) * is_valid
    cell_ids = lax.broadcasted_iota(jnp.int32, (cell_count, 1, 1), 0)
    return (picked[None] == cell_ids).astype(jnp.float32) * picked_weight[None]


def shards(samples, history, tile_cell, tile_weight):
    bl_size = lax.axis_size("bl")
    bl_index = lax.axis_index("bl")
    inputs_dev = samples.shape[0]
    spec_dev = samples.shape[1] // FRAME
    table = filter_table()
    frames = samples.reshape(inputs_dev, spec_dev, FRAME)
    last_frames = frames[:, spec_dev - (TAPS - 1) :, :]
    earlier = from_behind(last_frames, "bl", 1)
    earlier = jnp.where(bl_index == 0, history.reshape(inputs_dev, TAPS - 1, FRAME), earlier)
    extended = jnp.concatenate([earlier, frames], axis=1)
    accum = jnp.zeros((2 * CH, inputs_dev, spec_dev), jnp.float32)
    for tap_index in range(TAPS):
        accum = accum + jnp.einsum(
            "psn,nk->kps",
            extended[:, tap_index : tap_index + spec_dev],
            table[tap_index],
            preferred_element_type=jnp.float32,
        )
    spectra = accum.astype(jnp.bfloat16).reshape(2, CH, inputs_dev, spec_dev)
    turned = lax.all_to_all(spectra, "ct", split_axis=1, concat_axis=2, tiled=True)
    channels = turned.shape[1]
    inputs = turned.shape[2]
    blocks = inputs // BLOCK
    cell_count = CELL_DEV * bl_size
    weights = tile_weight * (1.0 / math.sqrt(SPECTRA))
    rows_each = blocks // bl_size
    shard_part = lax.all_gather(turned, "bl", axis=3, tiled=True)
    row_part = lax.dynamic_slice_in_dim(
        shard_part, bl_index * rows_each * BLOCK, rows_each * BLOCK, 2
    )
    products = jnp.einsum(
        "acps,bcqs->cabpq", row_part, shard_part, preferred_element_type=jnp.float32
    )
    visibility = jnp.stack(
        [products[:, 0, 0] + products[:, 1, 1], products[:, 1, 0] - products[:, 0, 1]], axis=1
    )
    visibility = visibility.reshape(channels, 2, rows_each, BLOCK, blocks, BLOCK)
    row_index = bl_index * rows_each + jnp.arange(rows_each, dtype=jnp.int32)
    col_index = jnp.arange(blocks, dtype=jnp.int32)
    is_valid = col_index[None, :] >= row_index[:, None]
    tri_index = (
        row_index[:, None] * blocks
        - row_index[:, None] * (row_index[:, None] - 1) // 2
        + col_index[None, :]
        - row_index[:, None]
    )
    tri_index = jnp.where(is_valid, tri_index, 0).reshape(-1)
    selector = cell_selector(
        tile_cell, weights, tri_index, is_valid.reshape(-1).astype(jnp.float32), cell_count
    )
    selector = selector.reshape(cell_count, channels, rows_each, blocks)
    cell_term = jnp.einsum(
        "ecmj,cxmpjq->ecxpq", selector, visibility, precision=lax.Precision.HIGHEST
    )
    return lax.psum_scatter(cell_term, "bl", scatter_dimension=0, tiled=True)


def solution(mesh):
    return jax.shard_map(
        shards,
        mesh=mesh,
        in_specs=(P("ct", "bl"), P("ct", None), P("ct", None), P("ct", None)),
        out_specs=P("bl", "ct", None, None, None),
        check_vma=False,
    )
```

profile of v0, /device:TPU:1, one launch (start us, length us, event | category | flops | bytes accessed | tf_op | source)
XLA Modules:
  0.0 138.1 jit_solution(12725136759354073979)
XLA Ops:
  6.5 0.0 all-gather.2.cloned.1.call-start
  6.5 1.0 copy.82
  7.6 3.9 %collective-permute-start = (bf16[8,3,512]{2,1,0:T(4,128)(2,1)S(1)}, bf16[8,3,512]{2,1,0:T(4,128)(2,1)S(1)}, u32[]{:S(2)}, u32[]{:S(2)}) collective-permute-start(bf16[8,3,512]{2,1,0:T(4,128)(2,1)S(1)} %slice.53), channel_id=1, source_target_pairs={{0,1},{1,2},{2,3},{4,5},{5,6},{6,7},{8,9},{9,10},{10,11},{12,13},{... | collective-permute-start | bytes 73736 | tf_op jit(solution)/shard_map/ppermute | solution.py:18
  11.6 2.1 %sine_negate_fusion = (f32[512,256]{1,0:T(8,128)S(1)}, f32[512,256]{1,0:T(8,128)S(1)}) fusion(), kind=kLoop, calls=%fused_computation.30 | loop fusion | flops 1966080 | bytes 1048576 | tf_op jit(solution)/shard_map/neg | solution.py:33
  13.6 0.1 fusion.32
  13.7 0.1 pad_maximum_fusion
  13.9 0.0 copy-start
  13.9 0.4 multiply_convert_fusion
  14.3 0.5 copy-done
  14.8 0.0 copy-start.1
  14.8 0.3 fusion.13
  15.2 0.4 copy-done.1
  15.6 0.0 collective-permute-done
  15.6 0.3 fusion.14
  16.0 0.3 convolution_add_fusion.1
  16.3 0.3 fusion.8
  16.6 0.1 reshape.299
  16.7 1.1 copy.52
  17.8 0.8 reshape.324
  18.6 32.0 %all_to_all.18 = bf16[128,2,512]{2,1,0:T(2,128)(2,1)S(1)} all-to-all(bf16[128,2,512]{2,1,0:T(2,128)(2,1)S(1)} %reshape.324), channel_id=1, replica_groups=mesh['ct'=128,'bl'=4] {'ct'}, dimensions={0} | all-to-all | bytes 524288 | tf_op jit(solution)/shard_map/all_to_all | solution.py:65
  50.6 0.5 reshape.325
  51.1 0.0 copy-start.2
  51.1 0.0 copy-start.3
  51.1 0.2 copy.81
  51.3 1.2 copy.55
  52.5 0.0 all-gather.2.cloned.1.call-update
  52.5 0.2 reduce-scatter.2.cloned.1.call-start
  52.8 0.1 add.224
  52.8 0.1 add.227
  52.9 0.1 ge.55
  53.0 0.1 ge.61
  53.1 0.1 ge.60
  53.2 0.0 copy-done.2
  53.2 0.1 copy.62
  53.3 0.6 gather_fusion.1
  53.9 0.1 copy.73
  53.9 0.0 copy-done.3
  53.9 0.1 copy.60
  54.0 0.6 gather_fusion
  54.6 0.1 copy.72
  54.7 0.1 fusion.41
  54.8 19.1 %all-gather.2.cloned.1.call-done = bf16[2,2,1024,128]{2,1,0,3:T(2,128)(2,1)} async-done(((bf16[2,2,1024,32]{2,1,0,3:T(2,128)(2,1)}), bf16[2,2,1024,128]{2,1,0,3:T(2,128)(2,1)}) %all-gather.2.cloned.1.call-update) | async-done | bytes 1048592 | tf_op jit(solution)/shard_map/all_gather | solution.py:72
  73.9 1.1 constant_dynamic-slice_fusion
  75.0 0.2 copy.74
  75.3 2.5 %convolution_bitcast_fusion = f32[2,2,2,256,1024]{3,4,1,2,0:T(8,128)S(1)} fusion(bf16[2,2,1024,128,1]{2,1,0,3,4:T(2,128)(2,1)} %bitcast.68, bf16[2,2,256,128]{3,2,0,1:T(8,128)(2,1)S(1)} %copy.74), kind=kOutput, calls=%fused_computation.7 | convolution fusion | flops 536870912 | bytes 9699328 | tf_op jit(solution)/shard_map/acps,bcqs->cabpq/dot_general | solution.py:76
  77.8 2.5 %slice_add_fusion = (f32[2,1,1,256,1024]{3,4,1,2,0:T(8,128)}, f32[2,1,1,256,1024]{3,4,1,2,0:T(8,128)}) fusion(f32[2,2,2,256,1024]{3,4,1,2,0:T(8,128)S(1)} %convolution_bitcast_fusion), kind=kLoop, calls=%fused_computation.9 | loop fusion | flops 1048576 | bytes 12582912 | tf_op jit(solution)/shard_map/add | solution.py:80
  80.3 2.3 %add.221 = f32[2,1,2,128,8,128]{3,2,5,4,0,1:T(2,128)S(1)} reshape(f32[2,1,1,256,1024]{3,4,1,2,0:T(8,128)} %get-tuple-element.5) | data formatting | bytes 4194304 | tf_op jit(solution)/shard_map/add | solution.py:80
  82.6 2.0 %copy.58 = f32[2,1,2,128,8,128]{5,4,2,3,1,0:T(8,128)} copy(f32[2,1,2,128,8,128]{3,2,5,4,0,1:T(2,128)S(1)} %add.221) | data formatting | bytes 4194304 | tf_op jit(solution)/shard_map/add | solution.py:80
  84.6 2.3 %sub.83 = f32[2,1,2,128,8,128]{3,2,5,4,0,1:T(2,128)S(1)} reshape(f32[2,1,1,256,1024]{3,4,1,2,0:T(8,128)} %get-tuple-element.6) | data formatting | bytes 4194304 | tf_op jit(solution)/shard_map/sub | solution.py:80
  86.9 2.0 %copy.59 = f32[2,1,2,128,8,128]{5,4,2,3,1,0:T(8,128)} copy(f32[2,1,2,128,8,128]{3,2,5,4,0,1:T(2,128)S(1)} %sub.83) | data formatting | bytes 4194304 | tf_op jit(solution)/shard_map/sub | solution.py:80
  89.0 4.0 %fusion.4 = f32[8,2,2,128,128]{4,0,3,2,1:T(8,128)S(1)} fusion(f32[2,1,2,128,8,128]{5,4,2,3,1,0:T(8,128)} %copy.59, f32[2,1,2,128,8,128]{5,4,2,3,1,0:T(8,128)} %copy.58, f32[2,2,8]{2,1,0:T(2,128)S(1)} %select_multiply_fusion, s32[2,2,8]{2,1,0:T(2,128)S(1)} %broadcast_select_fusion.1), kind=kOutput, calls=%fused_computation.10 | convolution fusion | flops 101712384 | bytes 6291712 | tf_op jit(solution)/shard_map/ecmj,cxmpjq->ecxpq/dot_general | solution.py:97
  93.0 1.7 %copy.64 = f32[8,2,2,128,128]{4,3,2,1,0:T(8,128)} copy(f32[8,2,2,128,128]{4,0,3,2,1:T(8,128)S(1)} %fusion.4) | data formatting | bytes 4194304 | tf_op jit(solution)/shard_map/ecmj,cxmpjq->ecxpq/transpose | solution.py:97
  94.7 0.0 reduce-scatter.2.cloned.1.call-update
  94.7 36.5 %reduce-scatter.2.cloned.1.call-done = f32[2,2,2,128,128]{4,3,2,1,0:T(8,128)} async-done(((f32[8,2,2,128,128]{4,3,2,1,0:T(8,128)}), f32[2,2,2,128,128]{4,3,2,1,0:T(8,128)}) %reduce-scatter.2.cloned.1.call-update) | async-done | bytes 524304 | tf_op jit(solution)/shard_map/reduce_scatter | solution.py:100
  (10 shorter events, 0.1 us)
Async XLA Ops:
  6.5 67.4 %all-gather.2.cloned.1.call-start = ((), (), s32[]{:S(2)}) async-start(), calls=%async_computation.2 | async-start | bytes 1310720 | tf_op jit(solution)/shard_map/all_gather | solution.py:72
  7.6 8.0 %collective-permute-start = (bf16[8,3,512]{2,1,0:T(4,128)(2,1)S(1)}, bf16[8,3,512]{2,1,0:T(4,128)(2,1)S(1)}, u32[]{:S(2)}, u32[]{:S(2)}) collective-permute-start(bf16[8,3,512]{2,1,0:T(4,128)(2,1)S(1)} %slice.53), channel_id=1, source_target_pairs={{0,1},{1,2},{2,3},{4,5},{5,6},{6,7},{8,9},{9,10},{10,11},{12,13},{... | collective-permute-start | bytes 73736 | tf_op jit(solution)/shard_map/ppermute | solution.py:18
  13.9 1.0 copy-start
  14.8 0.7 copy-start.1
  51.1 2.1 %copy-start.2 = (f32[2,36]{1,0:T(2,128)S(1)}, f32[2,36]{1,0:T(2,128)}, u32[]{:S(2)}) copy-start(f32[2,36]{1,0:T(2,128)} %param.7) | copy-start | bytes 868
  51.1 2.8 %copy-start.3 = (s32[2,36]{1,0:T(2,128)S(1)}, s32[2,36]{1,0:T(2,128)}, u32[]{:S(2)}) copy-start(s32[2,36]{1,0:T(2,128)} %param.6) | copy-start | bytes 868
  52.5 78.7 %reduce-scatter.2.cloned.1.call-start = ((), (), s32[]{:S(2)}) async-start(), calls=%async_computation.3 | async-start | bytes 2621440 | tf_op jit(solution)/shard_map/reduce_scatter | solution.py:100
Sparse Core Ops, SparseCore 0:
  52.6 21.2 all-gather.1
  94.9 36.3 reduce-scatter.1
where the time goes:
time: 138 us
  waiting for transfers between devices  55.6 us (40%)
  blocking collectives  32 us (23%)
  local copies, waits for them, and re-layouts  19.5 us (14%)
  between operations  13.6 us (10%)
  matrix products  7.79 us (6%)
  other arithmetic  5.36 us (4%)
  starting transfers between devices  4.17 us (3%)
    reduce_scatter x1, waiting for transfers between devices, shards(): return lax.psum_scatter(cell_term, 'bl', scatter_dimension=0, tiled=True)  36.5 us
    all_to_all x1, blocking collectives, shards(): lax.all_to_all(spectra, 'ct', split_axis=1, concat_axis=2, tiled=True)  32 us
    all_gather x1, waiting for transfers between devices, shards(): shard_part = lax.all_gather(turned, 'bl', axis=3, tiled=True)  19.1 us
    sub x2, local copies, waits for them, and re-layouts, shards(): products[:, 1, 0] - products[:, 0, 1]  4.33 us
    add x2, local copies, waits for them, and re-layouts, shards(): products[:, 0, 0] + products[:, 1, 1]  4.33 us
    dot_general x1, matrix products, shards(): jnp.einsum('ecmj,cxmpjq->ecxpq', selector, visibility, precision=lax.Prec...  4.02 us
    ppermute x1, starting transfers between devices, from_behind(): return lax.ppermute(value, axis, pairs)  3.95 us
    unnamed x13, local copies, waits for them, and re-layouts  3.65 us
  transfers between devices with their start and end apart: 3, of which 2 were waited for; matrix products, arithmetic and copies ran while one was open for 4% of the time, Pallas kernels for 0%

commit v1 on v0

--- a/solution.py
+++ b/solution.py
@@ -10,6 +10,28 @@
 SPECTRA = 128
 CELL_DEV = 2
 FRAME = 512
+
+
+def joined_along(blocks, dim):
+    blocks = jnp.moveaxis(blocks, 0, dim)
+    dims = blocks.shape
+    return blocks.reshape(*dims[:dim], dims[dim] * dims[dim + 1], *dims[dim + 2 :])
+
+
+def collect(shard, axis, dim):
+    peers = lax.axis_size(axis)
+    pairs = [(i, (i + 1) % peers) for i in range(peers)]
+    back = [(b, a) for a, b in pairs]
+    lower, upper = ([], [])
+    for step in range(peers - 1):
+        if step % 2 == 0:
+            lower.append(lax.ppermute(lower[-1] if lower else shard, axis, pairs))
+        else:
+            upper.append(lax.ppermute(upper[-1] if upper else shard, axis, back))
+    blocks = jnp.stack([*lower[::-1], shard, *upper])
+    shift = lax.axis_index(axis) - len(lower)
+    blocks = blocks[(jnp.arange(peers) - shift) % peers]
+    return joined_along(blocks, dim)
 
 
 def from_behind(value, axis, by):
@@ -69,7 +91,7 @@
     cell_count = CELL_DEV * bl_size
     weights = tile_weight * (1.0 / math.sqrt(SPECTRA))
     rows_each = blocks // bl_size
-    shard_part = lax.all_gather(turned, "bl", axis=3, tiled=True)
+    shard_part = collect(turned, "bl", 3)
     row_part = lax.dynamic_slice_in_dim(
         shard_part, bl_index * rows_each * BLOCK, rows_each * BLOCK, 2
     )

time: 138 us -> 127 us (0.920)
  blocking collectives: 32 us -> 0 us
  starting transfers between devices: 4.17 us -> 30.4 us
  waiting for transfers between devices: 55.6 us -> 51.4 us
    all_to_all x1 -> x0, blocking collectives: 32 us -> none  [shards(): lax.all_to_all(spectra, 'ct', split_axis=1, concat_axis=2, tiled=True)]
    all_gather x1 -> x0, waiting for transfers between devices: 19.1 us -> none  [shards(): shard_part = lax.all_gather(turned, 'bl', axis=3, tiled=True)]
    all_to_all x0 -> x1, starting transfers between devices: none -> 17.9 us  [shards(): lax.all_to_all(spectra, 'ct', split_axis=1, concat_axis=2, tiled=True)]
    all_to_all x0 -> x1, waiting for transfers between devices: none -> 14.1 us  [shards(): lax.all_to_all(spectra, 'ct', split_axis=1, concat_axis=2, tiled=True)]
    ppermute x0 -> x3, starting transfers between devices: none -> 8.57 us  [the longest x2 5.2 us: collect(): lower.append(lax.ppermute(lower[-1] if lower else shard, axis, pairs))]
    ppermute x0 -> x3, waiting for transfers between devices: none -> 6.94 us  [the longest x2 6.93 us: collect(): lower.append(lax.ppermute(lower[-1] if lower else shard, axis, pairs))]
    reduce_scatter x1, waiting for transfers between devices: 36.5 us -> 30.4 us  [shards(): return lax.psum_scatter(cell_term, 'bl', scatter_dimension=0, tiled=True)]
  transfers between devices with their start and end apart: 3 -> 6, of which waited for: 2 -> 4; matrix products, arithmetic and copies ran while one was open for 4% -> 4% of each run, Pallas kernels for 0% -> 0%
where the time goes in v1:
time: 127 us; the launch traced here: 126 us
  waiting for transfers between devices  51.4 us (40%)
  starting transfers between devices  30.4 us (24%)
  local copies, waits for them, and re-layouts  18.8 us (15%)
  between operations  13.7 us (11%)
  matrix products  6.56 us (5%)
  other arithmetic  5.52 us (4%)
    reduce_scatter x1, waiting for transfers between devices, shards(): return lax.psum_scatter(cell_term, 'bl', scatter_dimension=0, tiled=True)  30.4 us
    all_to_all x1, starting transfers between devices, shards(): lax.all_to_all(spectra, 'ct', split_axis=1, concat_axis=2, tiled=True)  17.9 us
    all_to_all x1, waiting for transfers between devices, shards(): lax.all_to_all(spectra, 'ct', split_axis=1, concat_axis=2, tiled=True)  14.1 us
    ppermute x2, waiting for transfers between devices, collect(): lower.append(lax.ppermute(lower[-1] if lower else shard, axis, pairs))  6.93 us
    ppermute x2, starting transfers between devices, collect(): lower.append(lax.ppermute(lower[-1] if lower else shard, axis, pairs))  5.2 us
    sub x2, local copies, waits for them, and re-layouts, shards(): products[:, 1, 0] - products[:, 0, 1]  4.33 us
    add x2, local copies, waits for them, and re-layouts, shards(): products[:, 0, 0] + products[:, 1, 1]  4.32 us
    dot_general x1, matrix products, shards(): jnp.einsum('ecmj,cxmpjq->ecxpq', selector, visibility, precision=lax.Prec...  4.02 us
  transfers between devices with their start and end apart: 6, of which 4 were waited for; matrix products, arithmetic and copies ran while one was open for 4% of the time, Pallas kernels for 0%

profile of v1, /device:TPU:1, one launch (start us, length us, event | category | flops | bytes accessed | tf_op | source)
XLA Modules:
  0.0 126.5 jit_solution(2275532657703800407)
XLA Ops:
  6.5 1.0 copy.84
  7.6 3.9 %collective-permute-start = (bf16[8,3,512]{2,1,0:T(4,128)(2,1)S(1)}, bf16[8,3,512]{2,1,0:T(4,128)(2,1)S(1)}, u32[]{:S(2)}, u32[]{:S(2)}) collective-permute-start(bf16[8,3,512]{2,1,0:T(4,128)(2,1)S(1)} %slice.55), channel_id=1, source_target_pairs={{0,1},{1,2},{2,3},{4,5},{5,6},{6,7},{8,9},{9,10},{10,11},{12,13},{... | collective-permute-start | bytes 73736 | tf_op jit(solution)/shard_map/ppermute | solution.py:40
  11.6 2.1 %sine_negate_fusion = (f32[512,256]{1,0:T(8,128)S(1)}, f32[512,256]{1,0:T(8,128)S(1)}) fusion(), kind=kLoop, calls=%fused_computation.33 | loop fusion | flops 1966080 | bytes 1048576 | tf_op jit(solution)/shard_map/neg | solution.py:55
  13.6 0.1 fusion.32
  13.7 0.1 pad_maximum_fusion
  13.9 0.0 copy-start
  13.9 0.4 multiply_convert_fusion
  14.3 0.5 copy-done
  14.8 0.0 copy-start.1
  14.8 0.3 fusion.13
  15.2 0.1 add.250
  15.2 0.1 add.253
  15.3 0.1 ge.55
  15.4 0.1 ge.61
  15.5 0.1 ge.60
  15.6 0.0 copy-done.1
  15.6 0.0 collective-permute-done
  15.7 0.3 fusion.14
  16.0 0.3 convolution_add_fusion.1
  16.3 0.3 fusion.8
  16.6 0.0 copy-start.2
  16.6 0.1 reshape.352
  16.7 1.1 copy.48
  17.8 1.5 %reshape.386 = bf16[128,2,512]{2,1,0:T(2,128)(2,1)} reshape(bf16[256,2,8,32]{3,2,1,0:T(8,128)(2,1)S(1)} %bitcast.82) | data formatting | bytes 524288
  19.3 17.9 %all-to-all-start = ((bf16[128,2,512]{2,1,0:T(2,128)(2,1)}), bf16[128,2,512]{2,1,0:T(2,128)(2,1)S(1)}, u32[]{:S(2)}, u32[]{:S(2)}) async-start(bf16[128,2,512]{2,1,0:T(2,128)(2,1)} %reshape.386), calls=%async_computation | async-start | bytes 524288 | tf_op jit(solution)/shard_map/all_to_all | solution.py:87
  37.2 0.0 reduce-scatter.2.cloned.1.call-start
  37.3 0.0 copy-done.2
  37.3 0.1 fusion.41
  37.4 0.0 copy-start.3
  37.4 14.1 %all-to-all-done = bf16[128,2,512]{2,1,0:T(2,128)(2,1)S(1)} async-done(((bf16[128,2,512]{2,1,0:T(2,128)(2,1)}), bf16[128,2,512]{2,1,0:T(2,128)(2,1)S(1)}, u32[]{:S(2)}, u32[]{:S(2)}) %all-to-all-start) | async-done | bytes 262176 | tf_op jit(solution)/shard_map/all_to_all | solution.py:87
  51.4 0.5 reshape.387
  52.0 0.2 copy.83
  52.1 0.3 copy.51
  52.5 3.1 %collective-permute-start.1 = (bf16[2,2,1024,32]{2,3,1,0:T(8,128)(2,1)S(1)}, bf16[2,2,1024,32]{2,3,1,0:T(8,128)(2,1)S(1)}, u32[]{:S(2)}, u32[]{:S(2)}) collective-permute-start(bf16[2,2,1024,32]{2,3,1,0:T(8,128)(2,1)S(1)} %copy.51), channel_id=1, source_target_pairs={{0,1},{1,2},{2,3},{3,0},{4,5},{5,6},{6,7},{7,4},{8,9},{9,10},{10,1... | collective-permute-start | bytes 786440 | tf_op jit(solution)/shard_map/ppermute | solution.py:28
  55.6 0.0 copy-done.3
  55.6 0.1 copy.60
  55.7 0.6 gather_fusion.1
  56.3 0.1 copy.73
  56.4 3.4 %collective-permute-start.3 = (bf16[2,2,1024,32]{2,3,1,0:T(8,128)(2,1)S(1)}, bf16[2,2,1024,32]{2,3,1,0:T(8,128)(2,1)S(1)}, u32[]{:S(2)}, u32[]{:S(2)}) collective-permute-start(bf16[2,2,1024,32]{2,3,1,0:T(8,128)(2,1)S(1)} %copy.51), channel_id=1, source_target_pairs={{1,0},{2,1},{3,2},{0,3},{5,4},{6,5},{7,6},{4,7},{9,8},{10,9},{11,1... | collective-permute-start | bytes 786440 | tf_op jit(solution)/shard_map/ppermute | solution.py:30
  59.8 1.8 %collective-permute-done.1 = bf16[2,2,1024,32]{2,3,1,0:T(8,128)(2,1)S(1)} collective-permute-done((bf16[2,2,1024,32]{2,3,1,0:T(8,128)(2,1)S(1)}, bf16[2,2,1024,32]{2,3,1,0:T(8,128)(2,1)S(1)}, u32[]{:S(2)}, u32[]{:S(2)}) %collective-permute-start.1) | collective-permute-done | bytes 262176 | tf_op jit(solution)/shard_map/ppermute | solution.py:28
  61.6 2.1 %collective-permute-start.2 = (bf16[2,2,1024,32]{2,3,1,0:T(8,128)(2,1)S(1)}, bf16[2,2,1024,32]{2,3,1,0:T(8,128)(2,1)S(1)}, u32[]{:S(2)}, u32[]{:S(2)}) collective-permute-start(bf16[2,2,1024,32]{2,3,1,0:T(8,128)(2,1)S(1)} %collective-permute-done.1), channel_id=1, source_target_pairs={{0,1},{1,2},{2,3},{3,0},{4,5},{5,6},{6,7},{7,4},{8,9},{9,10},{10,1... | collective-permute-start | bytes 786440 | tf_op jit(solution)/shard_map/ppermute | solution.py:28
  63.7 0.1 copy.62
  63.8 0.6 gather_fusion.2
  64.4 0.1 copy.74
  64.5 0.3 copy.54
  64.8 0.0 collective-permute-done.3
  64.8 5.1 %collective-permute-done.2 = bf16[2,2,1024,32]{2,3,1,0:T(8,128)(2,1)S(1)} collective-permute-done((bf16[2,2,1024,32]{2,3,1,0:T(8,128)(2,1)S(1)}, bf16[2,2,1024,32]{2,3,1,0:T(8,128)(2,1)S(1)}, u32[]{:S(2)}, u32[]{:S(2)}) %collective-permute-start.2) | collective-permute-done | bytes 262176 | tf_op jit(solution)/shard_map/ppermute | solution.py:28
  69.9 0.1 pad_maximum_fusion.1
  70.0 0.6 gather_fusion
  70.7 0.1 copy.55
  70.8 0.2 copy.75
  71.0 1.3 %convolution_bitcast_fusion = f32[2,2,2,256,1024]{3,4,1,2,0:T(8,128)S(1)} fusion(bf16[2,2,1024,128,1]{2,3,1,0,4:T(8,128)(2,1)S(1)} %bitcast.81, bf16[2,2,256,128]{3,2,0,1:T(8,128)(2,1)S(1)} %copy.75), kind=kOutput, calls=%fused_computation.8 | convolution fusion | flops 536870912 | bytes 9699328 | tf_op jit(solution)/shard_map/acps,bcqs->cabpq/dot_general | solution.py:98
  72.3 2.5 %slice_add_fusion = (f32[2,1,1,256,1024]{3,4,1,2,0:T(8,128)}, f32[2,1,1,256,1024]{3,4,1,2,0:T(8,128)}) fusion(f32[2,2,2,256,1024]{3,4,1,2,0:T(8,128)S(1)} %convolution_bitcast_fusion), kind=kLoop, calls=%fused_computation.10 | loop fusion | flops 1048576 | bytes 12582912 | tf_op jit(solution)/shard_map/add | solution.py:102
  74.8 2.3 %add.247 = f32[2,1,2,128,8,128]{3,2,5,4,0,1:T(2,128)S(1)} reshape(f32[2,1,1,256,1024]{3,4,1,2,0:T(8,128)} %get-tuple-element.5) | data formatting | bytes 4194304 | tf_op jit(solution)/shard_map/add | solution.py:102
  77.1 2.0 %copy.58 = f32[2,1,2,128,8,128]{5,4,2,3,1,0:T(8,128)} copy(f32[2,1,2,128,8,128]{3,2,5,4,0,1:T(2,128)S(1)} %add.247) | data formatting | bytes 4194304 | tf_op jit(solution)/shard_map/add | solution.py:102
  79.1 2.3 %sub.102 = f32[2,1,2,128,8,128]{3,2,5,4,0,1:T(2,128)S(1)} reshape(f32[2,1,1,256,1024]{3,4,1,2,0:T(8,128)} %get-tuple-element.6) | data formatting | bytes 4194304 | tf_op jit(solution)/shard_map/sub | solution.py:102
  81.4 2.0 %copy.59 = f32[2,1,2,128,8,128]{5,4,2,3,1,0:T(8,128)} copy(f32[2,1,2,128,8,128]{3,2,5,4,0,1:T(2,128)S(1)} %sub.102) | data formatting | bytes 4194304 | tf_op jit(solution)/shard_map/sub | solution.py:102
  83.4 4.0 %fusion.4 = f32[8,2,2,128,128]{4,0,3,2,1:T(8,128)S(1)} fusion(f32[2,1,2,128,8,128]{5,4,2,3,1,0:T(8,128)} %copy.59, f32[2,1,2,128,8,128]{5,4,2,3,1,0:T(8,128)} %copy.58, f32[2,2,8]{2,1,0:T(2,128)S(1)} %select_multiply_fusion, s32[2,2,8]{2,1,0:T(2,128)S(1)} %broadcast_select_fusion.1), kind=kOutput, calls=%fused_computation.11 | convolution fusion | flops 101712384 | bytes 6291712 | tf_op jit(solution)/shard_map/ecmj,cxmpjq->ecxpq/dot_general | solution.py:119
  87.5 1.7 %copy.64 = f32[8,2,2,128,128]{4,3,2,1,0:T(8,128)} copy(f32[8,2,2,128,128]{4,0,3,2,1:T(8,128)S(1)} %fusion.4) | data formatting | bytes 4194304 | tf_op jit(solution)/shard_map/ecmj,cxmpjq->ecxpq/transpose | solution.py:119
  89.2 0.0 reduce-scatter.2.cloned.1.call-update
  89.2 30.4 %reduce-scatter.2.cloned.1.call-done = f32[2,2,2,128,128]{4,3,2,1,0:T(8,128)} async-done(((f32[8,2,2,128,128]{4,3,2,1,0:T(8,128)}), f32[2,2,2,128,128]{4,3,2,1,0:T(8,128)}) %reduce-scatter.2.cloned.1.call-update) | async-done | bytes 524304 | tf_op jit(solution)/shard_map/reduce_scatter | solution.py:122
  (13 shorter events, 0.2 us)
Async XLA Ops:
  7.6 8.0 %collective-permute-start = (bf16[8,3,512]{2,1,0:T(4,128)(2,1)S(1)}, bf16[8,3,512]{2,1,0:T(4,128)(2,1)S(1)}, u32[]{:S(2)}, u32[]{:S(2)}) collective-permute-start(bf16[8,3,512]{2,1,0:T(4,128)(2,1)S(1)} %slice.55), channel_id=1, source_target_pairs={{0,1},{1,2},{2,3},{4,5},{5,6},{6,7},{8,9},{9,10},{10,11},{12,13},{... | collective-permute-start | bytes 73736 | tf_op jit(solution)/shard_map/ppermute | solution.py:40
  13.9 1.0 copy-start
  14.8 0.7 copy-start.1
  16.6 20.7 %copy-start.2 = (f32[2,36]{1,0:T(2,128)S(1)}, f32[2,36]{1,0:T(2,128)}, u32[]{:S(2)}) copy-start(f32[2,36]{1,0:T(2,128)} %param.7) | copy-start | bytes 868
  19.3 32.1 %all-to-all-start = ((bf16[128,2,512]{2,1,0:T(2,128)(2,1)}), bf16[128,2,512]{2,1,0:T(2,128)(2,1)S(1)}, u32[]{:S(2)}, u32[]{:S(2)}) async-start(bf16[128,2,512]{2,1,0:T(2,128)(2,1)} %reshape.386), calls=%async_computation | async-start | bytes 524288 | tf_op jit(solution)/shard_map/all_to_all | solution.py:87
  37.2 82.4 %reduce-scatter.2.cloned.1.call-start = ((), (), s32[]{:S(2)}) async-start(), calls=%async_computation.2 | async-start | bytes 2621440 | tf_op jit(solution)/shard_map/reduce_scatter | solution.py:122
  37.4 18.2 %copy-start.3 = (s32[2,36]{1,0:T(2,128)S(1)}, s32[2,36]{1,0:T(2,128)}, u32[]{:S(2)}) copy-start(s32[2,36]{1,0:T(2,128)} %param.6) | copy-start | bytes 868
  52.5 9.1 %collective-permute-start.1 = (bf16[2,2,1024,32]{2,3,1,0:T(8,128)(2,1)S(1)}, bf16[2,2,1024,32]{2,3,1,0:T(8,128)(2,1)S(1)}, u32[]{:S(2)}, u32[]{:S(2)}) collective-permute-start(bf16[2,2,1024,32]{2,3,1,0:T(8,128)(2,1)S(1)} %copy.51), channel_id=1, source_target_pairs={{0,1},{1,2},{2,3},{3,0},{4,5},{5,6},{6,7},{7,4},{8,9},{9,10},{10,1... | collective-permute-start | bytes 786440 | tf_op jit(solution)/shard_map/ppermute | solution.py:28
  56.4 8.4 %collective-permute-start.3 = (bf16[2,2,1024,32]{2,3,1,0:T(8,128)(2,1)S(1)}, bf16[2,2,1024,32]{2,3,1,0:T(8,128)(2,1)S(1)}, u32[]{:S(2)}, u32[]{:S(2)}) collective-permute-start(bf16[2,2,1024,32]{2,3,1,0:T(8,128)(2,1)S(1)} %copy.51), channel_id=1, source_target_pairs={{1,0},{2,1},{3,2},{0,3},{5,4},{6,5},{7,6},{4,7},{9,8},{10,9},{11,1... | collective-permute-start | bytes 786440 | tf_op jit(solution)/shard_map/ppermute | solution.py:30
  61.6 8.3 %collective-permute-start.2 = (bf16[2,2,1024,32]{2,3,1,0:T(8,128)(2,1)S(1)}, bf16[2,2,1024,32]{2,3,1,0:T(8,128)(2,1)S(1)}, u32[]{:S(2)}, u32[]{:S(2)}) collective-permute-start(bf16[2,2,1024,32]{2,3,1,0:T(8,128)(2,1)S(1)} %collective-permute-done.1), channel_id=1, source_target_pairs={{0,1},{1,2},{2,3},{3,0},{4,5},{5,6},{6,7},{7,4},{8,9},{9,10},{10,1... | collective-permute-start | bytes 786440 | tf_op jit(solution)/shard_map/ppermute | solution.py:28
Sparse Core Ops, SparseCore 0:
  89.3 30.2 reduce-scatter.1
